TPU v7x, 32 devices: a whole 2x2x4 slice. The times are simulated.
32 devices in a mesh: layer: 4 (over z), seq: 4 (over y, core), tile: 2 (over x).
Axes of the slice: x: 2, y: 2, z: 4, core: 2. Of those that a mesh axis runs over, the one named last changes fastest.
Arguments:
- activations: bfloat16 [16, 768, 4096], P('layer', 'seq', 'tile'), parts along dimension 0, may hold values from -6 to 6
- out_grads: bfloat16 [16, 768, 14336], P('layer', 'seq', 'tile'), parts along dimension 0, may hold values from -6 to 6
- proj_in: bfloat16 [16384, 128], P(('layer', 'tile')), parts along dimension 0, may hold values from -0.09375 to 0.09375
- proj_out: bfloat16 [57344, 256], P(('layer', 'tile')), parts along dimension 0, may hold values from -0.046875 to 0.046875
- seq_lengths: int32 [4], replicated, may hold values from 1 to 768, 1920 in all
- tile_map: int32 [8, 2], replicated, may hold values from 0 to 127, as said below
- prior_cov: float32 [32, 256, 256], P(('layer', 'seq', 'tile')), parts along dimension 0, may hold values from -6 to 6
Outputs:
- covariance: float32 [32, 256, 256], P(('layer', 'seq', 'tile')), parts along dimension 0
There are 4 independent parts, one for each index of `layer`. A program takes and returns all parts, laid end to end along the dimension named above; an argument that names none is the same for every part. Nothing has to cross between parts.
Inputs may be any that keep to these rules, and one draw needn't show every extreme that they name: `tile_map`: each row holds two feature block numbers, the first not above the second; rows may repeat.
All inputs are finite; a program needn't handle non-finite values.
Results may differ from a plain program's by a relative error of at most 0.0003.
Values sent between devices are 32-bit elements; how exact they have to be, the bound alone decides.
A program may use at most 192 MiB of HBM per device.

v0:
```python
import jax
import jax.numpy as jnp
from jax import lax
from jax.sharding import PartitionSpec as P


def project_tokens(act_rows, grad_rows, proj_in, proj_out):
    left_side = jnp.einsum("slc,ck->lsk", act_rows, proj_in, preferred_element_type=jnp.float32)
    right_side = jnp.einsum("slc,ck->lsk", grad_rows, proj_out, preferred_element_type=jnp.float32)
    return jnp.concatenate([left_side, right_side], axis=2)


def body(activations, out_grads, proj_in, proj_out, seq_lengths, tile_map, prior_cov):
    tiles_here = prior_cov.shape[0]
    block_size = prior_cov.shape[1]
    seq_count = activations.shape[0]
    tok_len = activations.shape[1]
    width_in = proj_in.shape[1]
    width_out = proj_out.shape[1]
    tile_count = lax.axis_size("tile")
    tok_rows = tok_len // tile_count
    whole_term = project_tokens(activations, out_grads, proj_in, proj_out)
    totals = lax.psum(whole_term, "tile")
    summed = lax.dynamic_slice_in_dim(totals, lax.axis_index("tile") * tok_rows, tok_rows, 0)
    positions = (
        lax.axis_index("seq") * tok_len
        + lax.axis_index("tile") * tok_rows
        + jnp.arange(tok_rows, dtype=jnp.int32)
    )
    token_mask = (positions[:, None] < seq_lengths[None, :]).astype(jnp.float32)
    token_weight = token_mask * lax.rsqrt(seq_lengths.astype(jnp.float32))[None, :]
    left_part = summed[:, :, :width_in]
    right_part = summed[:, :, width_in:] * token_weight[:, :, None]
    partial_value = jnp.einsum(
        "lsj,lsi->sji", right_part, left_part, precision=lax.Precision.HIGHEST
    )
    partial_value = partial_value.reshape(seq_count, width_out * width_in)
    offsets = jnp.arange(block_size, dtype=jnp.int32)
    features = lax.psum_scatter(partial_value, ("seq", "tile"), scatter_dimension=1, tiled=True)
    owner_index = lax.axis_index(("seq", "tile"))
    own_pairs = lax.dynamic_slice_in_dim(tile_map, owner_index * tiles_here, tiles_here, 0)
    shard_piece = lax.all_gather(features, ("seq", "tile"), axis=1, tiled=True)
    piece_width = shard_piece.shape[1]
    columns = own_pairs[:, :, None] * block_size + offsets
    inside = (columns >= 0) & (columns < piece_width)
    picked = jnp.take(shard_piece, jnp.clip(columns, 0, piece_width - 1), axis=1)
    picked = jnp.where(inside[None], picked, 0.0)
    chosen = jnp.transpose(picked, (1, 2, 0, 3))
    product = jnp.einsum(
        "kse,ksf->kef", chosen[:, 0], chosen[:, 1], precision=lax.Precision.HIGHEST
    )
    return prior_cov + product


def solution(mesh):
    return jax.shard_map(
        body,
        mesh=mesh,
        in_specs=(
            P("layer", "seq", "tile"),
            P("layer", "seq", "tile"),
            P(("layer", "tile"), None),
            P(("layer", "tile"), None),
            P(),
            P(),
            P(("layer", "seq", "tile"), None, None),
        ),
        out_specs=P(("layer", "seq", "tile"), None, None),
        check_vma=False,
    )
```

profile of v0, /device:TPU:0, one launch (start us, length us, event | category | flops | bytes accessed | tf_op | source)
XLA Modules:
  0.0 351.4 jit_solution(6703392492950285449)
XLA Ops:
  6.5 0.0 copy-start
  6.5 0.0 all-reduce.2.cloned.1.call-start
  6.5 0.0 copy-start.1
  6.5 7.0 %fusion.2 = f32[192,4,256]{2,0,1:T(8,128)S(1)} fusion(bf16[4,192,7168]{2,1,0:T(8,128)(2,1)} %param.8, bf16[7168,256]{1,0:T(8,128)(2,1)} %param.10), kind=kOutput, calls=%fused_computation.3 | convolution fusion | flops 2818572288 | bytes 15466496 | tf_op jit(solution)/shard_map/slc,ck->lsk/dot_general | solution.py:9
  13.6 0.0 copy-done
  13.6 0.0 copy-done.1
  13.6 0.0 copy-start.3
  13.6 1.0 convolution_bitcast_fusion
  14.6 1.1 pad_maximum_fusion
  15.7 0.0 all-reduce.2.cloned.1.call-update
  15.8 0.0 reduce-scatter.2.cloned.1.call-start
  15.8 0.0 copy-done.3
  15.9 0.1 compare_select_fusion.2
  15.9 45.6 %all-reduce.2.cloned.1.call-done = f32[192,4,384]{2,0,1:T(8,128)} async-done(((f32[192,4,384]{2,0,1:T(8,128)}), f32[192,4,384]{2,0,1:T(8,128)}) %all-reduce.2.cloned.1.call-update) | async-done | bytes 1179664 | tf_op jit(solution)/shard_map/psum | solution.py:23
  61.5 3.0 fusion.7
  64.5 9.5 %copy.10 = f32[4,256,128]{0,2,1:T(8,128)} copy(f32[4,256,128]{2,1,0:T(8,128)} %fusion.7) | data formatting | bytes 1048576 | tf_op jit(solution)/shard_map/reshape | solution.py:37
  74.0 0.0 copy-start.2
  74.0 0.0 reduce-scatter.2.cloned.1.call-update
  74.0 0.6 copy-done.2
  74.7 0.2 multiply_reduce_fusion
  74.9 0.1 fusion.10
  75.0 0.1 compare_and_fusion.1
  75.0 115.1 %reduce-scatter.2.cloned.1.call-done = f32[4,4096]{0,1:T(8,128)} async-done(((f32[4,32768]{0,1:T(8,128)}), f32[4,4096]{0,1:T(8,128)}) %reduce-scatter.2.cloned.1.call-update) | async-done | bytes 65552 | tf_op jit(solution)/shard_map/reduce_scatter | solution.py:39
  190.1 145.4 %all_gather.3 = f32[4,32768]{0,1:T(8,128)} all-gather(f32[4,4096]{0,1:T(8,128)} %reduce-scatter.2.cloned.1.call-done), channel_id=1, replica_groups=mesh['layer'=4,'seq'=4,'tile'=2] {'seq','tile'}, dimensions={1}, use_global_device_ids=true | all-gather | bytes 589824 | tf_op jit(solution)/shard_map/all_gather | solution.py:42
  335.6 6.8 %gather_fusion = f32[512,4]{1,0:T(8,128)S(1)} fusion(f32[4,32768]{0,1:T(8,128)} %all_gather.3, s32[1024]{0:T(1024)S(1)} %pad_clamp_fusion), kind=kCustom, calls=%fused_computation | custom fusion | bytes 18432 | tf_op jit(solution)/shard_map/jit(_take)/gather | solution.py:46
  342.4 0.2 select_bitcast_fusion
  342.6 2.0 fusion.5
  (4 shorter events, 0.0 us)
Async XLA Ops:
  6.5 7.1 %copy-start = (bf16[4,192,2048]{2,1,0:T(8,128)(2,1)S(1)}, bf16[4,192,2048]{2,1,0:T(8,128)(2,1)}, u32[]{:S(2)}) copy-start(bf16[4,192,2048]{2,1,0:T(8,128)(2,1)} %param.7) | copy-start | bytes 9437188
  6.5 55.0 %all-reduce.2.cloned.1.call-start = ((), (), s32[]{:S(2)}) async-start(), calls=%async_computation.1 | async-start | bytes 2359296 | tf_op jit(solution)/shard_map/psum | solution.py:23
  6.5 7.1 %copy-start.1 = (bf16[2048,128]{1,0:T(8,128)(2,1)S(1)}, bf16[2048,128]{1,0:T(8,128)(2,1)}, u32[]{:S(2)}) copy-start(bf16[2048,128]{1,0:T(8,128)(2,1)} %param.9) | copy-start | bytes 1572868
  13.6 2.2 copy-start.3
  15.8 174.4 %reduce-scatter.2.cloned.1.call-start = ((), (), s32[]{:S(2)}) async-start(), calls=%async_computation.2 | async-start | bytes 18874368 | tf_op jit(solution)/shard_map/reduce_scatter | solution.py:39
  74.0 0.7 copy-start.2
Sparse Core Ops, SparseCore 0:
  15.9 45.5 all-reduce.1
  74.1 115.9 reduce-scatter.1
where the time goes:
time: 352 us; the launch traced here: 351 us
  waiting for transfers between devices  161 us (46%)
  blocking collectives  145 us (41%)
  local copies, waits for them, and re-layouts  17 us (5%)
  between operations  13.5 us (4%)
  matrix products  13 us (4%)
    all_gather x1, blocking collectives, body(): shard_piece = lax.all_gather(features, ('seq', 'tile'), axis=1, tiled=True)  145 us
    reduce_scatter x1, waiting for transfers between devices, body(): lax.psum_scatter(partial_value, ('seq', 'tile'), scatter_dimension=1, til...  115 us
    psum x1, waiting for transfers between devices, body(): totals = lax.psum(whole_term, 'tile')  45.6 us
    reshape x1, local copies, waits for them, and re-layouts, body(): partial_value = partial_value.reshape(seq_count, width_out * width_in)  9.52 us
    dot_general x1, matrix products, project_tokens(): jnp.einsum('slc,ck->lsk', grad_rows, proj_out, preferred_element_type=jnp...  7.04 us
  transfers between devices with their start and end apart: 2, of which 2 were waited for; matrix products, arithmetic and copies ran while one was open for 0% of the time, Pallas kernels for 0%

commit v1 on v0

v1 whole, which is shorter than its diff:
```python
import functools

import jax
import jax.numpy as jnp
from jax import lax
from jax.experimental import pallas as pl
from jax.experimental.pallas import tpu as pltpu
from jax.sharding import PartitionSpec as P

MESH = pl.DeviceIdType.MESH
F32 = jnp.float32
BF16 = jnp.bfloat16


def split_two(x):
    high = x.astype(BF16)
    return high, (x - high.astype(F32)).astype(BF16)


def dot_nt(a, b):
    return lax.dot_general(a, b, (((1,), (1,)), ((), ())), preferred_element_type=F32)


def kernel(
    seq_axis, tile_axis,
    lengths, tile_map, act_hbm, grad_hbm, pin_hbm, pout_hbm, prior_hbm,
    out_ref,
    act_v, grad_v, pin_v, pout_v, prior_v,
    picked, picked_in, acts, parts, parts_in, summed,
    load_sem, pick_send, pick_recv, part_send, part_recv,
):
    seqs, tok, _ = act_v.shape
    tiles = tile_map.shape[0]
    group = seq_axis * tile_axis
    here = tiles // group
    rows = 4 * tiles
    seq_me = lax.axis_index("seq")
    tile_me = lax.axis_index("tile")
    me = seq_me * tile_axis + tile_me

    loads = [pltpu.make_async_copy(pout_hbm, pout_v, load_sem.at[0])]
    for s in range(seqs):
        loads.append(pltpu.make_async_copy(grad_hbm.at[s], grad_v.at[s], load_sem.at[1 + s]))
    loads.append(pltpu.make_async_copy(pin_hbm, pin_v, load_sem.at[1 + seqs]))
    loads.append(pltpu.make_async_copy(act_hbm, act_v, load_sem.at[2 + seqs]))
    loads.append(pltpu.make_async_copy(prior_hbm, prior_v, load_sem.at[3 + seqs]))
    for load in loads:
        load.start()

    def peer(d):
        other = lax.rem(me + d, group)
        return other, {"seq": lax.div(other, tile_axis), "tile": lax.rem(other, tile_axis)}

    barrier = pltpu.get_barrier_semaphore()
    for d in range(1, group):
        pl.semaphore_signal(barrier, inc=1, device_id=peer(d)[1], device_id_type=MESH)

    width_out = pout_v.shape[1]
    width_in = pin_v.shape[1]
    per_block = out_ref.shape[1] // width_in
    row = lax.broadcasted_iota(jnp.int32, (rows, width_out), 0)
    column = lax.broadcasted_iota(jnp.int32, (rows, width_out), 1)
    wanted = jnp.zeros((rows, width_out), jnp.int32)
    for k in range(tiles):
        for side in range(2):
            wanted = jnp.where(row // per_block == 2 * k + side, tile_map[k, side], wanted)
    select = (column == wanted * per_block + row % per_block).astype(F32).astype(BF16)

    loads[0].wait()
    picks = []
    for s in range(seqs):
        loads[1 + s].wait()
        projected = jnp.dot(grad_v[s], pout_v[...], preferred_element_type=F32)
        high, low = split_two(projected)
        picked[s] = dot_nt(select, high) + dot_nt(select, low)
        if s == 0:
            pl.semaphore_wait(barrier, group - 1)
        for d in range(1, tile_axis):
            copy = pltpu.make_async_remote_copy(
                src_ref=picked.at[s],
                dst_ref=picked_in.at[d - 1, s],
                send_sem=pick_send.at[d - 1, s],
                recv_sem=pick_recv.at[d - 1, s],
                device_id={"tile": lax.rem(tile_me + d, tile_axis)},
                device_id_type=MESH,
            )
            copy.start()
            picks.append(copy)

    loads[1 + seqs].wait()
    loads[2 + seqs].wait()
    for s in range(seqs):
        acts[s] = jnp.dot(act_v[s], pin_v[...], preferred_element_type=F32)

    position = seq_me * tok + lax.broadcasted_iota(jnp.int32, (1, tok), 1)
    for s in range(seqs):
        total = picked[s]
        for d in range(1, tile_axis):
            picks[s * (tile_axis - 1) + d - 1].wait_recv()
            total = total + picked_in[d - 1, s]
        length = jnp.full((1, tok), lengths[s], jnp.int32)
        weight = jnp.where(position < length, lax.rsqrt(length.astype(F32)), 0.0)
        part = jnp.dot(
            total * weight, acts[s], precision=lax.Precision.HIGHEST, preferred_element_type=F32
        )
        for k in range(tiles):
            parts[k, 4 * s : 4 * s + 4, :] = part[4 * k : 4 * k + 4, :]

    moves = []
    for d in range(1, group):
        other, where = peer(d)
        copy = pltpu.make_async_remote_copy(
            src_ref=parts.at[pl.ds(other * here, here)],
            dst_ref=parts_in.at[d - 1],
            send_sem=part_send.at[d - 1],
            recv_sem=part_recv.at[d - 1],
            device_id=where,
            device_id_type=MESH,
        )
        copy.start()
        moves.append(copy)

    loads[3 + seqs].wait()
    total = parts[pl.ds(me * here, here)]
    for d in range(1, group):
        moves[d - 1].wait_recv()
        total = total + parts_in[d - 1]
    summed[...] = total
    for k in range(here):
        pieces = [summed[k, pl.ds(c, seqs, stride=4), :] for c in range(4)]
        left = jnp.concatenate(pieces[:2], axis=1)
        right = jnp.concatenate(pieces[2:], axis=1)
        product = lax.dot_general(
            left, right, (((0,), (0,)), ((), ())),
            precision=lax.Precision.HIGHEST, preferred_element_type=F32,
        )
        out_ref[k] = prior_v[k] + product
    for copy in picks:
        copy.wait_send()
    for copy in moves:
        copy.wait_send()


def body(seq_axis, tile_axis, activations, out_grads, proj_in, proj_out, seq_lengths, tile_map, prior_cov):
    seqs, tok, _ = activations.shape
    tiles = tile_map.shape[0]
    group = seq_axis * tile_axis
    here = prior_cov.shape[0]
    width_in = proj_in.shape[1]
    others = max(tile_axis - 1, 1)
    smem = pl.BlockSpec(memory_space=pltpu.SMEM)
    hbm = pl.BlockSpec(memory_space=pl.ANY)
    vmem = pl.BlockSpec(memory_space=pltpu.VMEM)
    return pl.pallas_call(
        functools.partial(kernel, seq_axis, tile_axis),
        out_shape=jax.ShapeDtypeStruct(prior_cov.shape, F32),
        in_specs=[smem, smem, hbm, hbm, hbm, hbm, hbm],
        out_specs=vmem,
        scratch_shapes=[
            pltpu.VMEM(activations.shape, BF16),
            pltpu.VMEM(out_grads.shape, BF16),
            pltpu.VMEM(proj_in.shape, BF16),
            pltpu.VMEM(proj_out.shape, BF16),
            pltpu.VMEM(prior_cov.shape, F32),
            pltpu.VMEM((seqs, 4 * tiles, tok), F32),
            pltpu.VMEM((others, seqs, 4 * tiles, tok), F32),
            pltpu.VMEM((seqs, tok, width_in), F32),
            pltpu.VMEM((tiles, 4 * seqs, width_in), F32),
            pltpu.VMEM((group - 1, here, 4 * seqs, width_in), F32),
            pltpu.VMEM((here, 4 * seqs, width_in), F32),
            pltpu.SemaphoreType.DMA((4 + seqs,)),
            pltpu.SemaphoreType.DMA((others, seqs)),
            pltpu.SemaphoreType.DMA((others, seqs)),
            pltpu.SemaphoreType.DMA((group - 1,)),
            pltpu.SemaphoreType.DMA((group - 1,)),
        ],
        compiler_params=pltpu.CompilerParams(
            collective_id=0, has_side_effects=True, vmem_limit_bytes=48 * 1024 * 1024
        ),
        name="grad_tiles",
    )(seq_lengths, tile_map, activations, out_grads, proj_in, proj_out, prior_cov)


def solution(mesh):
    return jax.shard_map(
        functools.partial(body, mesh.shape["seq"], mesh.shape["tile"]),
        mesh=mesh,
        in_specs=(
            P("layer", "seq", "tile"),
            P("layer", "seq", "tile"),
            P(("layer", "tile"), None),
            P(("layer", "tile"), None),
            P(),
            P(),
            P(("layer", "seq", "tile"), None, None),
        ),
        out_specs=P(("layer", "seq", "tile"), None, None),
        check_vma=False,
    )
```

time: 352 us -> 25.8 us (0.07)
  waiting for transfers between devices: 161 us -> 0 us
  blocking collectives: 145 us -> 0 us
  Pallas kernels: 0 us -> 19.6 us
  between operations: 13.5 us -> 0.01 us
  matrix products: 13 us -> 0 us
  local copies, waits for them, and re-layouts: 17 us -> 5.99 us
    all_gather x1 -> x0, blocking collectives: 145 us -> none  [body(): shard_piece = lax.all_gather(features, ('seq', 'tile'), axis=1, tiled=True)]
    reduce_scatter x1 -> x0, waiting for transfers between devices: 115 us -> none  [body(): lax.psum_scatter(partial_value, ('seq', 'tile'), scatter_dimension=1, til...]
    psum x1 -> x0, waiting for transfers between devices: 45.6 us -> none  [body(): totals = lax.psum(whole_term, 'tile')]
    pallas_call x0 -> x1, Pallas kernels: none -> 19.6 us  [body(): pl.pallas_call(functools.partial(kernel, seq_axis, tile_axis), out_shape=...]
    dot_general x4 -> x0, matrix products: 13 us -> none  [the longest x1 7.04 us: project_tokens(): jnp.einsum('slc,ck->lsk', grad_rows, proj_out, preferred_element_type=jnp...]
    reshape x1 -> x0, local copies, waits for them, and re-layouts: 9.52 us -> none  [body(): partial_value = partial_value.reshape(seq_count, width_out * width_in)]
    gather x1 -> x0, local copies, waits for them, and re-layouts: 6.8 us -> none  [body(): jnp.take(shard_piece, jnp.clip(columns, 0, piece_width - 1), axis=1)]
    unnamed x9 -> x10, local copies, waits for them, and re-layouts: 0.67 us -> 5.99 us
  transfers between devices with their start and end apart: 2 -> 0, of which waited for: 2 -> 0; matrix products, arithmetic and copies ran while one was open for 0% -> 0% of each run, Pallas kernels for 0% -> 0%
where the time goes in v1:
time: 25.8 us; the launch traced here: 25.6 us
  Pallas kernels  19.6 us (76%)
  local copies, waits for them, and re-layouts  5.99 us (23%)
    pallas_call x1, Pallas kernels, body(): pl.pallas_call(functools.partial(kernel, seq_axis, tile_axis), out_shape=...  19.6 us
    unnamed x10, local copies, waits for them, and re-layouts  5.99 us

profile of v1, /device:TPU:0, one launch (start us, length us, event | category | flops | bytes accessed | tf_op | source)
XLA Modules:
  0.0 25.6 jit_solution(15974940885151651528)
XLA Ops:
  0.0 0.8 %copy.8.tile_map = s32[8,2]{1,0:T(8,128)S(1)} copy(s32[8,2]{0,1:T(2,128)} %param.12) | data formatting | bytes 128 | tf_op args[5]
  0.8 0.0 copy-start
  0.8 1.9 %copy-done = bf16[4,192,2048]{2,1,0:T(8,128)(2,1)S(1)} copy-done((bf16[4,192,2048]{2,1,0:T(8,128)(2,1)S(1)}, bf16[4,192,2048]{2,1,0:T(8,128)(2,1)}, u32[]{:S(2)}) %copy-start) | copy-done | bytes 3145752
  2.6 0.0 copy-start.1
  2.6 1.0 %copy-done.1 = bf16[2048,128]{1,0:T(8,128)(2,1)S(1)} copy-done((bf16[2048,128]{1,0:T(8,128)(2,1)S(1)}, bf16[2048,128]{1,0:T(8,128)(2,1)}, u32[]{:S(2)}) %copy-start.1) | copy-done | bytes 524312
  3.7 0.0 copy-start.2
  3.7 0.9 %copy-done.2 = f32[1,256,256]{2,1,0:T(8,128)S(1)} copy-done((f32[1,256,256]{2,1,0:T(8,128)S(1)}, f32[1,256,256]{2,1,0:T(8,128)}, u32[]{:S(2)}) %copy-start.2) | copy-done | bytes 262168
  4.6 0.0 copy-start.3
  4.6 0.7 %copy-done.3 = s32[4]{0:T(128)S(1)} copy-done((s32[4]{0:T(128)S(1)}, s32[4]{0:T(128)}, u32[]{:S(2)}) %copy-start.3) | copy-done | bytes 40
  5.3 19.6 %grad_tiles.1 = f32[1,256,256]{2,1,0:T(8,128)S(1)} custom-call(s32[4]{0:T(128)S(1)} %copy-done.3, s32[8,2]{1,0:T(8,128)S(1)} %copy.8.tile_map, bf16[4,192,2048]{2,1,0:T(8,128)(2,1)S(1)} %copy-done, bf16[4,192,7168]{2,1,0:T(8,128)(2,1)} %grad_hbm.1, bf16[2048,128]{1,0:T(8,128)(2,1)S(1)} %copy-done.1, bf16[7168,256]{1,0:T(8,128)(2,1)} %pout_hbm.1, ...), custom_call_target="tpu_custom_call" | custom-call | tf_op jit(solution)/shard_map/grad_tiles/pallas_call | solution.py:154
  24.9 0.7 %copy.10 = f32[1,256,256]{2,1,0:T(8,128)} copy(f32[1,256,256]{2,1,0:T(8,128)S(1)} %grad_tiles.1) | data formatting | bytes 524288
Async XLA Ops:
  0.8 1.9 %copy-start = (bf16[4,192,2048]{2,1,0:T(8,128)(2,1)S(1)}, bf16[4,192,2048]{2,1,0:T(8,128)(2,1)}, u32[]{:S(2)}) copy-start(bf16[4,192,2048]{2,1,0:T(8,128)(2,1)} %act_hbm.1) | copy-start | bytes 9437188
  2.6 1.0 %copy-start.1 = (bf16[2048,128]{1,0:T(8,128)(2,1)S(1)}, bf16[2048,128]{1,0:T(8,128)(2,1)}, u32[]{:S(2)}) copy-start(bf16[2048,128]{1,0:T(8,128)(2,1)} %pin_hbm.1) | copy-start | bytes 1572868
  3.7 0.9 %copy-start.2 = (f32[1,256,256]{2,1,0:T(8,128)S(1)}, f32[1,256,256]{2,1,0:T(8,128)}, u32[]{:S(2)}) copy-start(f32[1,256,256]{2,1,0:T(8,128)} %prior_hbm.1) | copy-start | bytes 786436
  4.6 0.7 %copy-start.3 = (s32[4]{0:T(128)S(1)}, s32[4]{0:T(128)}, u32[]{:S(2)}) copy-start(s32[4]{0:T(128)} %lengths.1) | copy-start | bytes 52

commit v2 on v1

--- a/solution.py
+++ b/solution.py
@@ -26,11 +26,14 @@
     lengths, tile_map, act_hbm, grad_hbm, pin_hbm, pout_hbm, prior_hbm,
     out_ref,
     act_v, grad_v, pin_v, pout_v, prior_v,
-    picked, picked_in, acts, parts, parts_in, summed,
-    load_sem, pick_send, pick_recv, part_send, part_recv,
+    total_v, picked, picked_in, acts, parts, parts_in, summed,
+    pout_sem, grad_sem, act_sem, rest_sem, pick_send, pick_recv, part_send, part_recv,
 ):
-    seqs, tok, _ = act_v.shape
-    tiles = tile_map.shape[0]
+    seqs, tok, width = act_v.shape
+    chunks, deep, width_out = pout_v.shape
+    halves = act_sem.shape[0]
+    per = seqs // halves
+    tiles = tile_map.shape[1]
     group = seq_axis * tile_axis
     here = tiles // group
     rows = 4 * tiles
@@ -38,14 +41,34 @@
     tile_me = lax.axis_index("tile")
     me = seq_me * tile_axis + tile_me
 
-    loads = [pltpu.make_async_copy(pout_hbm, pout_v, load_sem.at[0])]
-    for s in range(seqs):
-        loads.append(pltpu.make_async_copy(grad_hbm.at[s], grad_v.at[s], load_sem.at[1 + s]))
-    loads.append(pltpu.make_async_copy(pin_hbm, pin_v, load_sem.at[1 + seqs]))
-    loads.append(pltpu.make_async_copy(act_hbm, act_v, load_sem.at[2 + seqs]))
-    loads.append(pltpu.make_async_copy(prior_hbm, prior_v, load_sem.at[3 + seqs]))
-    for load in loads:
-        load.start()
+    def load_pout(k):
+        return pltpu.make_async_copy(
+            pout_hbm.at[pl.ds(pl.multiple_of(k * deep, 128), deep)], pout_v.at[k], pout_sem.at[k]
+        )
+
+    def load_grad(h, k):
+        return pltpu.make_async_copy(
+            grad_hbm.at[pl.ds(h * per, per), :, pl.ds(pl.multiple_of(k * deep, 128), deep)],
+            grad_v.at[k, pl.ds(h * per, per)],
+            grad_sem.at[h, k],
+        )
+
+    def load_act(h):
+        return pltpu.make_async_copy(
+            act_hbm.at[pl.ds(h * per, per)], act_v.at[pl.ds(h * per, per)], act_sem.at[h]
+        )
+
+    load_pin = pltpu.make_async_copy(pin_hbm, pin_v, rest_sem.at[0])
+    load_prior = pltpu.make_async_copy(prior_hbm, prior_v, rest_sem.at[1])
+    for h in range(halves):
+        for k in range(chunks):
+            if h == 0:
+                load_pout(k).start()
+            load_grad(h, k).start()
+    load_pin.start()
+    for h in range(halves):
+        load_act(h).start()
+    load_prior.start()
 
     def peer(d):
         other = lax.rem(me + d, group)
@@ -55,7 +78,6 @@
     for d in range(1, group):
         pl.semaphore_signal(barrier, inc=1, device_id=peer(d)[1], device_id_type=MESH)
 
-    width_out = pout_v.shape[1]
     width_in = pin_v.shape[1]
     per_block = out_ref.shape[1] // width_in
     row = lax.broadcasted_iota(jnp.int32, (rows, width_out), 0)
@@ -63,46 +85,60 @@
     wanted = jnp.zeros((rows, width_out), jnp.int32)
     for k in range(tiles):
         for side in range(2):
-            wanted = jnp.where(row // per_block == 2 * k + side, tile_map[k, side], wanted)
+            wanted = jnp.where(row // per_block == 2 * k + side, tile_map[side, k], wanted)
     select = (column == wanted * per_block + row % per_block).astype(F32).astype(BF16)
 
-    loads[0].wait()
     picks = []
-    for s in range(seqs):
-        loads[1 + s].wait()
-        projected = jnp.dot(grad_v[s], pout_v[...], preferred_element_type=F32)
-        high, low = split_two(projected)
-        picked[s] = dot_nt(select, high) + dot_nt(select, low)
-        if s == 0:
+    for h in range(halves):
+        total_v[...] = jnp.zeros_like(total_v)
+
+        @pl.loop(0, chunks)
+        def _(k):
+            if h == 0:
+                load_pout(k).wait()
+            load_grad(h, k).wait()
+            block = grad_v[k, pl.ds(h * per, per)].reshape(per * tok, deep)
+            total_v[...] += jnp.dot(block, pout_v[k], preferred_element_type=F32)
+
+        for i in range(per):
+            high, low = split_two(total_v[i * tok : (i + 1) * tok, :])
+            picked[h * per + i] = dot_nt(select, high) + dot_nt(select, low)
+        if h == 0:
             pl.semaphore_wait(barrier, group - 1)
         for d in range(1, tile_axis):
             copy = pltpu.make_async_remote_copy(
-                src_ref=picked.at[s],
-                dst_ref=picked_in.at[d - 1, s],
-                send_sem=pick_send.at[d - 1, s],
-                recv_sem=pick_recv.at[d - 1, s],
+                src_ref=picked.at[pl.ds(h * per, per)],
+                dst_ref=picked_in.at[d - 1, pl.ds(h * per, per)],
+                send_sem=pick_send.at[d - 1, h],
+                recv_sem=pick_recv.at[d - 1, h],
                 device_id={"tile": lax.rem(tile_me + d, tile_axis)},
                 device_id_type=MESH,
             )
             copy.start()
             picks.append(copy)
 
-    loads[1 + seqs].wait()
-    loads[2 + seqs].wait()
-    for s in range(seqs):
-        acts[s] = jnp.dot(act_v[s], pin_v[...], preferred_element_type=F32)
+    load_pin.wait()
+    for h in range(halves):
+        load_act(h).wait()
+        block = act_v[pl.ds(h * per, per)].reshape(per * tok, width)
+        projected = jnp.dot(block, pin_v[...], preferred_element_type=F32)
+        acts[pl.ds(h * per, per)] = jnp.concatenate(split_two(projected), axis=1).reshape(
+            per, tok, 2 * width_in
+        )
 
     position = seq_me * tok + lax.broadcasted_iota(jnp.int32, (1, tok), 1)
     for s in range(seqs):
         total = picked[s]
         for d in range(1, tile_axis):
-            picks[s * (tile_axis - 1) + d - 1].wait_recv()
+            if s % per == 0:
+                picks[s // per * (tile_axis - 1) + d - 1].wait_recv()
             total = total + picked_in[d - 1, s]
         length = jnp.full((1, tok), lengths[s], jnp.int32)
         weight = jnp.where(position < length, lax.rsqrt(length.astype(F32)), 0.0)
-        part = jnp.dot(
-            total * weight, acts[s], precision=lax.Precision.HIGHEST, preferred_element_type=F32
-        )
+        high, low = split_two(total * weight)
+        both = jnp.dot(high, acts[s], preferred_element_type=F32)
+        part = both[:, :width_in] + both[:, width_in:]
+        part = part + jnp.dot(low, acts[s, :, :width_in], preferred_element_type=F32)
         for k in range(tiles):
             parts[k, 4 * s : 4 * s + 4, :] = part[4 * k : 4 * k + 4, :]
 
@@ -120,7 +156,7 @@
         copy.start()
         moves.append(copy)
 
-    loads[3 + seqs].wait()
+    load_prior.wait()
     total = parts[pl.ds(me * here, here)]
     for d in range(1, group):
         moves[d - 1].wait_recv()
@@ -148,6 +184,10 @@
     here = prior_cov.shape[0]
     width_in = proj_in.shape[1]
     others = max(tile_axis - 1, 1)
+    halves = 2 if seqs % 2 == 0 else 1
+    depth = proj_out.shape[0]
+    chunks = next(c for c in (4, 2, 1) if depth % (256 * c) == 0 or c == 1)
+    deep = depth // chunks
     smem = pl.BlockSpec(memory_space=pltpu.SMEM)
     hbm = pl.BlockSpec(memory_space=pl.ANY)
     vmem = pl.BlockSpec(memory_space=pltpu.VMEM)
@@ -158,27 +198,31 @@
         out_specs=vmem,
         scratch_shapes=[
             pltpu.VMEM(activations.shape, BF16),
-            pltpu.VMEM(out_grads.shape, BF16),
+            pltpu.VMEM((chunks, seqs, tok, deep), BF16),
             pltpu.VMEM(proj_in.shape, BF16),
-            pltpu.VMEM(proj_out.shape, BF16),
+            pltpu.VMEM((chunks, deep, proj_out.shape[1]), BF16),
             pltpu.VMEM(prior_cov.shape, F32),
+            pltpu.VMEM((seqs // halves * tok, proj_out.shape[1]), F32),
             pltpu.VMEM((seqs, 4 * tiles, tok), F32),
             pltpu.VMEM((others, seqs, 4 * tiles, tok), F32),
-            pltpu.VMEM((seqs, tok, width_in), F32),
+            pltpu.VMEM((seqs, tok, 2 * width_in), BF16),
             pltpu.VMEM((tiles, 4 * seqs, width_in), F32),
             pltpu.VMEM((group - 1, here, 4 * seqs, width_in), F32),
             pltpu.VMEM((here, 4 * seqs, width_in), F32),
-            pltpu.SemaphoreType.DMA((4 + seqs,)),
-            pltpu.SemaphoreType.DMA((others, seqs)),
-            pltpu.SemaphoreType.DMA((others, seqs)),
+            pltpu.SemaphoreType.DMA((chunks,)),
+            pltpu.SemaphoreType.DMA((halves, chunks)),
+            pltpu.SemaphoreType.DMA((halves,)),
+            pltpu.SemaphoreType.DMA((2,)),
+            pltpu.SemaphoreType.DMA((others, halves)),
+            pltpu.SemaphoreType.DMA((others, halves)),
             pltpu.SemaphoreType.DMA((group - 1,)),
             pltpu.SemaphoreType.DMA((group - 1,)),
         ],
         compiler_params=pltpu.CompilerParams(
-            collective_id=0, has_side_effects=True, vmem_limit_bytes=48 * 1024 * 1024
+            collective_id=0, has_side_effects=True, vmem_limit_bytes=64 * 1024 * 1024
         ),
         name="grad_tiles",
-    )(seq_lengths, tile_map, activations, out_grads, proj_in, proj_out, prior_cov)
+    )(seq_lengths, tile_map.T, activations, out_grads, proj_in, proj_out, prior_cov)
 
 
 def solution(mesh):

time: 25.8 us -> 21.6 us (0.84)
  local copies, waits for them, and re-layouts: 5.99 us -> 1.67 us
    unnamed x10 -> x1, local copies, waits for them, and re-layouts: 5.99 us -> 1.67 us
where the time goes in v2:
time: 21.6 us; the launch traced here: 21.4 us
  Pallas kernels  19.8 us (92%)
  local copies, waits for them, and re-layouts  1.67 us (8%)
    pallas_call x1, Pallas kernels, body(): pl.pallas_call(functools.partial(kernel, seq_axis, tile_axis), out_shape=...  19.8 us
    unnamed x1, local copies, waits for them, and re-layouts  1.67 us

profile of v2, /device:TPU:0, one launch (start us, length us, event | category | flops | bytes accessed | tf_op | source)
XLA Modules:
  0.0 21.4 jit_solution(5411433897355576288)
XLA Ops:
  0.0 19.8 %grad_tiles.1 = f32[1,256,256]{2,1,0:T(8,128)} custom-call(s32[4]{0:T(128)} %lengths.1, s32[2,8]{1,0:T(2,128)} %bitcast.1, bf16[4,192,2048]{2,1,0:T(8,128)(2,1)} %act_hbm.1, bf16[4,192,7168]{2,1,0:T(8,128)(2,1)} %grad_hbm.1, bf16[2048,128]{1,0:T(8,128)(2,1)} %pin_hbm.1, bf16[7168,256]{1,0:T(8,128)(2,1)} %pout_hbm.1, f32[1,256,256]{2,1,0:T(8,128)} %prior_hbm.1), custom_call_target="tpu_custom_call" | custom-call | tf_op jit(solution)/shard_map/grad_tiles/pallas_call | solution.py:194
  19.8 1.7 %copy.9 = f32[1,256,256]{2,1,0:T(8,128)} copy(f32[1,256,256]{2,1,0:T(8,128)} %grad_tiles.1) | data formatting | bytes 524288

commit v3 on v2

v3 whole, which is shorter than its diff:
```python
import functools

import jax
import jax.numpy as jnp
from jax import lax
from jax.experimental import pallas as pl
from jax.experimental.pallas import tpu as pltpu
from jax.sharding import PartitionSpec as P

MESH = pl.DeviceIdType.MESH
F32 = jnp.float32
BF16 = jnp.bfloat16


def split_two(x):
    high = x.astype(BF16)
    return high, (x - high.astype(F32)).astype(BF16)


def dot(a, b):
    return jnp.dot(a, b, preferred_element_type=F32)


def kernel(
    seq_axis, tile_axis,
    lengths_hbm, map_hbm, act_hbm, grad_hbm, pin_hbm, pout_hbm, prior_hbm,
    out_ref,
    lengths, tile_map, act_v, grad_v, pin_v, pout_v, prior_v,
    select_v, total_v, picked, picked_in, acts, parts, parts_in, stacked,
    pout_sem, grad_sem, act_sem, rest_sem, pick_send, pick_recv, part_send, part_recv,
):
    seqs, tok, width = act_v.shape
    chunks, deep, width_out = pout_v.shape
    halves = act_sem.shape[0]
    sub = tok // halves
    tiles = tile_map.shape[1]
    width_in = pin_v.shape[1]
    per_block = out_ref.shape[1] // width_in
    sides = 2 * per_block
    rows = sides * seqs
    lanes = tiles * rows
    group = seq_axis * tile_axis
    here = tiles // group
    seq_me = lax.axis_index("seq")
    tile_me = lax.axis_index("tile")
    me = seq_me * tile_axis + tile_me

    def load_pout(k):
        return pltpu.make_async_copy(
            pout_hbm.at[pl.ds(pl.multiple_of(k * deep, 128), deep)], pout_v.at[k], pout_sem.at[k]
        )

    def load_grad(h, k):
        return pltpu.make_async_copy(
            grad_hbm.at[:, pl.ds(h * sub, sub), pl.ds(pl.multiple_of(k * deep, 128), deep)],
            grad_v.at[k, :, pl.ds(h * sub, sub)],
            grad_sem.at[h, k],
        )

    def load_act(h):
        return pltpu.make_async_copy(
            act_hbm.at[:, pl.ds(h * sub, sub)], act_v.at[:, pl.ds(h * sub, sub)], act_sem.at[h]
        )

    load_map = pltpu.make_async_copy(map_hbm, tile_map, rest_sem.at[0])
    load_lengths = pltpu.make_async_copy(lengths_hbm, lengths, rest_sem.at[1])
    load_pin = pltpu.make_async_copy(pin_hbm, pin_v, rest_sem.at[2])
    load_prior = pltpu.make_async_copy(prior_hbm, prior_v, rest_sem.at[3])
    load_map.start()
    load_lengths.start()
    for h in range(halves):
        for k in range(chunks):
            if h == 0:
                load_pout(k).start()
            load_grad(h, k).start()
    load_pin.start()
    for h in range(halves):
        load_act(h).start()
    load_prior.start()

    def peer(d):
        other = lax.rem(me + d, group)
        return other, {"seq": lax.div(other, tile_axis), "tile": lax.rem(other, tile_axis)}

    barrier = pltpu.get_barrier_semaphore()
    for d in range(1, group):
        pl.semaphore_signal(barrier, inc=1, device_id=peer(d)[1], device_id_type=MESH)

    load_map.wait()
    load_lengths.wait()
    lane = lax.broadcasted_iota(jnp.int32, (1, lanes), 1)
    side = lane // seqs % sides
    wanted = jnp.zeros((1, lanes), jnp.int32)
    for k in range(tiles):
        block = jnp.where(side < per_block, tile_map[0, k], tile_map[1, k])
        wanted = jnp.where(lane // rows == k, block, wanted)
    wanted = wanted * per_block + side % per_block
    length = jnp.zeros((1, lanes), jnp.int32)
    for s in range(seqs):
        length = jnp.where(lane % seqs == s, lengths[s], length)
    scale = lax.rsqrt(length.astype(F32))
    column = lax.broadcasted_iota(jnp.int32, (width_out, lanes), 0)
    for s in range(seqs):
        match = jnp.where(column == wanted, 1.0, 0.0) * jnp.where(lane % seqs == s, 1.0, 0.0)
        select_v[s * width_out : (s + 1) * width_out, :] = match.astype(BF16)

    picks = []
    for h in range(halves):
        total_v[...] = jnp.zeros_like(total_v)

        @pl.loop(0, chunks)
        def _(k):
            if h == 0:
                load_pout(k).wait()
            load_grad(h, k).wait()
            block = grad_v[k, :, pl.ds(h * sub, sub)].reshape(seqs * sub, deep)
            total_v[...] += dot(block, pout_v[k])

        high, low = split_two(total_v[...])
        stack = jnp.concatenate(
            [
                jnp.concatenate([x[s * sub : (s + 1) * sub] for s in range(seqs)], axis=1)
                for x in (high, low)
            ],
            axis=0,
        )
        both = dot(stack, select_v[...])
        picked[h] = both[:sub] + both[sub:]
        if h == 0:
            pl.semaphore_wait(barrier, group - 1)
        for d in range(1, tile_axis):
            copy = pltpu.make_async_remote_copy(
                src_ref=picked.at[h],
                dst_ref=picked_in.at[d - 1, h],
                send_sem=pick_send.at[d - 1, h],
                recv_sem=pick_recv.at[d - 1, h],
                device_id={"tile": lax.rem(tile_me + d, tile_axis)},
                device_id_type=MESH,
            )
            copy.start()
            picks.append(copy)

    load_pin.wait()
    for h in range(halves):
        load_act(h).wait()
        block = act_v[:, pl.ds(h * sub, sub)].reshape(seqs * sub, width)
        split = split_two(dot(block, pin_v[...]))
        for j in range(2):
            for s in range(seqs):
                at = (j * seqs + s) * width_in
                acts[h, :, at : at + width_in] = split[j][s * sub : (s + 1) * sub]

    partial = jnp.zeros((lanes, seqs * width_in), F32)
    for h in range(halves):
        total = picked[h]
        for d in range(1, tile_axis):
            picks[h * (tile_axis - 1) + d - 1].wait_recv()
            total = total + picked_in[d - 1, h]
        position = seq_me * tok + h * sub + lax.broadcasted_iota(jnp.int32, (sub, lanes), 0)
        total = jnp.where(position < length, total * scale, 0.0)
        high, low = split_two(total.T)
        both = dot(high, acts[h])
        partial = partial + both[:, : seqs * width_in] + both[:, seqs * width_in :]
        partial = partial + dot(low, acts[h, :, : seqs * width_in])
    row = lax.broadcasted_iota(jnp.int32, (lanes, width_in), 0)
    own = jnp.zeros((lanes, width_in), F32)
    for s in range(seqs):
        own = jnp.where(row % seqs == s, partial[:, s * width_in : (s + 1) * width_in], own)
    parts[...] = own.reshape(tiles, rows, width_in)

    moves = []
    for d in range(1, group):
        other, where = peer(d)
        copy = pltpu.make_async_remote_copy(
            src_ref=parts.at[pl.ds(other * here, here)],
            dst_ref=parts_in.at[d - 1],
            send_sem=part_send.at[d - 1],
            recv_sem=part_recv.at[d - 1],
            device_id=where,
            device_id_type=MESH,
        )
        copy.start()
        moves.append(copy)

    load_prior.wait()
    total = parts[pl.ds(me * here, here)]
    for d in range(1, group):
        moves[d - 1].wait_recv()
        total = total + parts_in[d - 1]
    for k in range(here):
        pieces = [total[k, c * seqs : (c + 1) * seqs, :] for c in range(sides)]
        wide = [
            jnp.concatenate(pieces[:per_block], axis=1),
            jnp.concatenate(pieces[per_block:], axis=1),
        ]
        split = [[x.astype(F32) for x in split_two(side)] for side in wide]
        for j, part in enumerate((0, 1, 0)):
            stacked[0, j * seqs : (j + 1) * seqs, :] = split[0][part]
        for j, part in enumerate((0, 0, 1)):
            stacked[1, j * seqs : (j + 1) * seqs, :] = split[1][part]
        left = stacked[0].T.astype(BF16)
        out_ref[k] = prior_v[k] + dot(left, stacked[1].astype(BF16))
    for copy in picks:
        copy.wait_send()
    for copy in moves:
        copy.wait_send()


def body(seq_axis, tile_axis, activations, out_grads, proj_in, proj_out, seq_lengths, tile_map, prior_cov):
    seqs, tok, _ = activations.shape
    tiles = tile_map.shape[0]
    group = seq_axis * tile_axis
    here, block_size, _ = prior_cov.shape
    width_in = proj_in.shape[1]
    depth, width_out = proj_out.shape
    rows = 2 * (block_size // width_in) * seqs
    others = max(tile_axis - 1, 1)
    halves = 2 if tok % 32 == 0 else 1
    chunks = next(c for c in (4, 2, 1) if depth % (256 * c) == 0 or c == 1)
    sub, deep = tok // halves, depth // chunks
    hbm = pl.BlockSpec(memory_space=pltpu.HBM)
    vmem = pl.BlockSpec(memory_space=pltpu.VMEM)
    return pl.pallas_call(
        functools.partial(kernel, seq_axis, tile_axis),
        out_shape=jax.ShapeDtypeStruct(prior_cov.shape, F32),
        in_specs=[hbm] * 7,
        out_specs=vmem,
        scratch_shapes=[
            pltpu.SMEM(seq_lengths.shape, jnp.int32),
            pltpu.SMEM(tile_map.shape[::-1], jnp.int32),
            pltpu.VMEM(activations.shape, BF16),
            pltpu.VMEM((chunks, seqs, tok, deep), BF16),
            pltpu.VMEM(proj_in.shape, BF16),
            pltpu.VMEM((chunks, deep, width_out), BF16),
            pltpu.VMEM(prior_cov.shape, F32),
            pltpu.VMEM((seqs * width_out, tiles * rows), BF16),
            pltpu.VMEM((seqs * sub, width_out), F32),
            pltpu.VMEM((halves, sub, tiles * rows), F32),
            pltpu.VMEM((others, halves, sub, tiles * rows), F32),
            pltpu.VMEM((halves, sub, 2 * seqs * width_in), BF16),
            pltpu.VMEM((tiles, rows, width_in), F32),
            pltpu.VMEM((group - 1, here, rows, width_in), F32),
            pltpu.VMEM((2, 3 * seqs, block_size), F32),
            pltpu.SemaphoreType.DMA((chunks,)),
            pltpu.SemaphoreType.DMA((halves, chunks)),
            pltpu.SemaphoreType.DMA((halves,)),
            pltpu.SemaphoreType.DMA((4,)),
            pltpu.SemaphoreType.DMA((others, halves)),
            pltpu.SemaphoreType.DMA((others, halves)),
            pltpu.SemaphoreType.DMA((group - 1,)),
            pltpu.SemaphoreType.DMA((group - 1,)),
        ],
        compiler_params=pltpu.CompilerParams(
            collective_id=0, has_side_effects=True, vmem_limit_bytes=40 * 1024 * 1024
        ),
        name="grad_tiles",
    )(seq_lengths, tile_map.T, activations, out_grads, proj_in, proj_out, prior_cov)


def solution(mesh):
    return jax.shard_map(
        functools.partial(body, mesh.shape["seq"], mesh.shape["tile"]),
        mesh=mesh,
        in_specs=(
            P("layer", "seq", "tile"),
            P("layer", "seq", "tile"),
            P(("layer", "tile"), None),
            P(("layer", "tile"), None),
            P(),
            P(),
            P(("layer", "seq", "tile"), None, None),
        ),
        out_specs=P(("layer", "seq", "tile"), None, None),
        check_vma=False,
    )
```

time: 21.6 us -> 23.9 us (1.11)
  local copies, waits for them, and re-layouts: 1.67 us -> 7.96 us
  Pallas kernels: 19.8 us -> 15.6 us
    unnamed x1 -> x13, local copies, waits for them, and re-layouts: 1.67 us -> 7.96 us
    pallas_call x1, Pallas kernels: 19.8 us -> 15.6 us  [body(): pl.pallas_call(functools.partial(kernel, seq_axis, tile_axis), out_shape=...]
where the time goes in v3:
time: 23.9 us; the launch traced here: 23.6 us
  Pallas kernels  15.6 us (65%)
  local copies, waits for them, and re-layouts  7.96 us (33%)
    pallas_call x1, Pallas kernels, body(): pl.pallas_call(functools.partial(kernel, seq_axis, tile_axis), out_shape=...  15.6 us
    unnamed x13, local copies, waits for them, and re-layouts  7.96 us

profile of v3, /device:TPU:0, one launch (start us, length us, event | category | flops | bytes accessed | tf_op | source)
XLA Modules:
  0.0 23.6 jit_solution(11603080938121739966)
XLA Ops:
  0.0 0.0 copy-start
  0.0 2.0 %copy-done = bf16[7168,256]{1,0:T(8,128)(2,1)S(1)} copy-done((bf16[7168,256]{1,0:T(8,128)(2,1)S(1)}, bf16[7168,256]{1,0:T(8,128)(2,1)}, u32[]{:S(2)}) %copy-start) | copy-done | bytes 3670040
  2.0 0.0 copy-start.1
  2.0 1.9 %copy-done.1 = bf16[4,192,2048]{2,1,0:T(8,128)(2,1)S(1)} copy-done((bf16[4,192,2048]{2,1,0:T(8,128)(2,1)S(1)}, bf16[4,192,2048]{2,1,0:T(8,128)(2,1)}, u32[]{:S(2)}) %copy-start.1) | copy-done | bytes 3145752
  3.9 0.0 copy-start.2
  3.9 1.0 %copy-done.2 = bf16[2048,128]{1,0:T(8,128)(2,1)S(1)} copy-done((bf16[2048,128]{1,0:T(8,128)(2,1)S(1)}, bf16[2048,128]{1,0:T(8,128)(2,1)}, u32[]{:S(2)}) %copy-start.2) | copy-done | bytes 524312
  5.0 0.0 copy-start.3
  5.0 0.9 %copy-done.3 = f32[1,256,256]{2,1,0:T(8,128)S(1)} copy-done((f32[1,256,256]{2,1,0:T(8,128)S(1)}, f32[1,256,256]{2,1,0:T(8,128)}, u32[]{:S(2)}) %copy-start.3) | copy-done | bytes 262168
  5.9 0.0 copy-start.4
  5.9 0.7 %copy-done.4 = s32[8,2]{0,1:T(2,128)S(1)} copy-done((s32[8,2]{0,1:T(2,128)S(1)}, s32[8,2]{0,1:T(2,128)}, u32[]{:S(2)}) %copy-start.4) | copy-done | bytes 88
  6.6 0.0 copy-start.5
  6.6 0.7 %copy-done.5 = s32[4]{0:T(128)S(1)} copy-done((s32[4]{0:T(128)S(1)}, s32[4]{0:T(128)}, u32[]{:S(2)}) %copy-start.5) | copy-done | bytes 40
  7.3 15.6 %grad_tiles.1 = f32[1,256,256]{2,1,0:T(8,128)S(1)} custom-call(s32[4]{0:T(128)S(1)} %copy-done.5, s32[2,8]{1,0:T(2,128)S(1)} %bitcast.1, bf16[4,192,2048]{2,1,0:T(8,128)(2,1)S(1)} %copy-done.1, bf16[4,192,7168]{2,1,0:T(8,128)(2,1)} %grad_hbm.1, bf16[2048,128]{1,0:T(8,128)(2,1)S(1)} %copy-done.2, bf16[7168,256]{1,0:T(8,128)(2,1)S(1)} %copy-done, ...), custom_call_target="tpu_custom_call" | custom-call | tf_op jit(solution)/shard_map/grad_tiles/pallas_call | solution.py:223
  22.9 0.7 %copy.9 = f32[1,256,256]{2,1,0:T(8,128)} copy(f32[1,256,256]{2,1,0:T(8,128)S(1)} %grad_tiles.1) | data formatting | bytes 524288
Async XLA Ops:
  0.0 2.0 %copy-start = (bf16[7168,256]{1,0:T(8,128)(2,1)S(1)}, bf16[7168,256]{1,0:T(8,128)(2,1)}, u32[]{:S(2)}) copy-start(bf16[7168,256]{1,0:T(8,128)(2,1)} %pout_hbm.1) | copy-start | bytes 11010052
  2.0 1.9 %copy-start.1 = (bf16[4,192,2048]{2,1,0:T(8,128)(2,1)S(1)}, bf16[4,192,2048]{2,1,0:T(8,128)(2,1)}, u32[]{:S(2)}) copy-start(bf16[4,192,2048]{2,1,0:T(8,128)(2,1)} %act_hbm.1) | copy-start | bytes 9437188
  3.9 1.0 %copy-start.2 = (bf16[2048,128]{1,0:T(8,128)(2,1)S(1)}, bf16[2048,128]{1,0:T(8,128)(2,1)}, u32[]{:S(2)}) copy-start(bf16[2048,128]{1,0:T(8,128)(2,1)} %pin_hbm.1) | copy-start | bytes 1572868
  5.0 0.9 %copy-start.3 = (f32[1,256,256]{2,1,0:T(8,128)S(1)}, f32[1,256,256]{2,1,0:T(8,128)}, u32[]{:S(2)}) copy-start(f32[1,256,256]{2,1,0:T(8,128)} %prior_hbm.1) | copy-start | bytes 786436
  5.9 0.7 %copy-start.4 = (s32[8,2]{0,1:T(2,128)S(1)}, s32[8,2]{0,1:T(2,128)}, u32[]{:S(2)}) copy-start(s32[8,2]{0,1:T(2,128)} %param.12) | copy-start | bytes 196
  6.6 0.7 %copy-start.5 = (s32[4]{0:T(128)S(1)}, s32[4]{0:T(128)}, u32[]{:S(2)}) copy-start(s32[4]{0:T(128)} %lengths_hbm.1) | copy-start | bytes 52

commit v4 on v3

--- a/solution.py
+++ b/solution.py
@@ -222,7 +222,7 @@
     vmem = pl.BlockSpec(memory_space=pltpu.VMEM)
     return pl.pallas_call(
         functools.partial(kernel, seq_axis, tile_axis),
-        out_shape=jax.ShapeDtypeStruct(prior_cov.shape, F32),
+        out_shape=pltpu.VMEM(prior_cov.shape, F32),
         in_specs=[hbm] * 7,
         out_specs=vmem,
         scratch_shapes=[
@@ -251,10 +251,15 @@
             pltpu.SemaphoreType.DMA((group - 1,)),
         ],
         compiler_params=pltpu.CompilerParams(
-            collective_id=0, has_side_effects=True, vmem_limit_bytes=40 * 1024 * 1024
+            collective_id=0, has_side_effects=True, vmem_limit_bytes=48 * 1024 * 1024
         ),
         name="grad_tiles",
-    )(seq_lengths, tile_map.T, activations, out_grads, proj_in, proj_out, prior_cov)
+    )(
+        *(
+            pltpu.with_memory_space_constraint(x, pltpu.HBM)
+            for x in (seq_lengths, tile_map.T, activations, out_grads, proj_in, proj_out, prior_cov)
+        )
+    )
 
 
 def solution(mesh):

time: 23.9 us -> 17 us (0.71)
  local copies, waits for them, and re-layouts: 7.96 us -> 0.71 us
  Pallas kernels: 15.6 us -> 16.1 us
    unnamed x13 -> x1, local copies, waits for them, and re-layouts: 7.96 us -> 0.71 us
    pallas_call x1, Pallas kernels: 15.6 us -> 16.1 us  [body(): pl.pallas_call(functools.partial(kernel, seq_axis, tile_axis), out_shape=...]
where the time goes in v4:
time: 17 us; the launch traced here: 16.8 us
  Pallas kernels  16.1 us (95%)
  local copies, waits for them, and re-layouts  0.71 us (4%)
    pallas_call x1, Pallas kernels, body(): pl.pallas_call(functools.partial(kernel, seq_axis, tile_axis), out_shape=...  16.1 us
    unnamed x1, local copies, waits for them, and re-layouts  0.71 us

profile of v4, /device:TPU:0, one launch (start us, length us, event | category | flops | bytes accessed | tf_op | source)
XLA Modules:
  0.0 16.8 jit_solution(14285055521436470048)
XLA Ops:
  0.0 16.1 %grad_tiles.1 = f32[1,256,256]{2,1,0:T(8,128)S(1)} custom-call(s32[4]{0:T(128)} %lengths_hbm.1, s32[2,8]{1,0:T(2,128)} %bitcast.1, bf16[4,192,2048]{2,1,0:T(8,128)(2,1)} %act_hbm.1, bf16[4,192,7168]{2,1,0:T(8,128)(2,1)} %grad_hbm.1, bf16[2048,128]{1,0:T(8,128)(2,1)} %pin_hbm.1, bf16[7168,256]{1,0:T(8,128)(2,1)} %pout_hbm.1, f32[1,256,256]{2,1,0:T(8,128)} %prior_hbm.1), custom_call_target="tpu_custom_call" | custom-call | tf_op jit(solution)/shard_map/grad_tiles/pallas_call | solution.py:223
  16.1 0.7 %copy.9 = f32[1,256,256]{2,1,0:T(8,128)} copy(f32[1,256,256]{2,1,0:T(8,128)S(1)} %grad_tiles.1) | data formatting | bytes 524288

commit v5 on v4

--- a/solution.py
+++ b/solution.py
@@ -10,6 +10,7 @@
 MESH = pl.DeviceIdType.MESH
 F32 = jnp.float32
 BF16 = jnp.bfloat16
+AHEAD = 3
 
 
 def split_two(x):
@@ -50,11 +51,9 @@
             pout_hbm.at[pl.ds(pl.multiple_of(k * deep, 128), deep)], pout_v.at[k], pout_sem.at[k]
         )
 
-    def load_grad(h, k):
+    def load_grad(k):
         return pltpu.make_async_copy(
-            grad_hbm.at[:, pl.ds(h * sub, sub), pl.ds(pl.multiple_of(k * deep, 128), deep)],
-            grad_v.at[k, :, pl.ds(h * sub, sub)],
-            grad_sem.at[h, k],
+            grad_hbm.at[:, :, pl.ds(pl.multiple_of(k * deep, 128), deep)], grad_v.at[k], grad_sem.at[k]
         )
 
     def load_act(h):
@@ -68,15 +67,9 @@
     load_prior = pltpu.make_async_copy(prior_hbm, prior_v, rest_sem.at[3])
     load_map.start()
     load_lengths.start()
-    for h in range(halves):
-        for k in range(chunks):
-            if h == 0:
-                load_pout(k).start()
-            load_grad(h, k).start()
-    load_pin.start()
-    for h in range(halves):
-        load_act(h).start()
-    load_prior.start()
+    for k in range(min(AHEAD, chunks)):
+        load_pout(k).start()
+        load_grad(k).start()
 
     def peer(d):
         other = lax.rem(me + d, group)
@@ -104,26 +97,32 @@
         match = jnp.where(column == wanted, 1.0, 0.0) * jnp.where(lane % seqs == s, 1.0, 0.0)
         select_v[s * width_out : (s + 1) * width_out, :] = match.astype(BF16)
 
+    total_v[...] = jnp.zeros_like(total_v)
+
+    @pl.loop(0, chunks)
+    def _(k):
+        load_pout(k).wait()
+        load_grad(k).wait()
+
+        @pl.when(k + AHEAD < chunks)
+        def _():
+            load_pout(k + AHEAD).start()
+            load_grad(k + AHEAD).start()
+
+        @pl.when(k == max(chunks - AHEAD, 0))
+        def _():
+            load_pin.start()
+            for h in range(halves):
+                load_act(h).start()
+            load_prior.start()
+
+        total_v[...] += dot(grad_v[k].reshape(seqs * tok, deep), pout_v[k])
+
     picks = []
     for h in range(halves):
-        total_v[...] = jnp.zeros_like(total_v)
-
-        @pl.loop(0, chunks)
-        def _(k):
-            if h == 0:
-                load_pout(k).wait()
-            load_grad(h, k).wait()
-            block = grad_v[k, :, pl.ds(h * sub, sub)].reshape(seqs * sub, deep)
-            total_v[...] += dot(block, pout_v[k])
-
-        high, low = split_two(total_v[...])
-        stack = jnp.concatenate(
-            [
-                jnp.concatenate([x[s * sub : (s + 1) * sub] for s in range(seqs)], axis=1)
-                for x in (high, low)
-            ],
-            axis=0,
-        )
+        begin = [s * tok + h * sub for s in range(seqs)]
+        wide = jnp.concatenate([total_v[at : at + sub, :] for at in begin], axis=1)
+        stack = jnp.concatenate(split_two(wide), axis=0)
         both = dot(stack, select_v[...])
         picked[h] = both[:sub] + both[sub:]
         if h == 0:
@@ -216,7 +215,7 @@
     rows = 2 * (block_size // width_in) * seqs
     others = max(tile_axis - 1, 1)
     halves = 2 if tok % 32 == 0 else 1
-    chunks = next(c for c in (4, 2, 1) if depth % (256 * c) == 0 or c == 1)
+    chunks = next(c for c in (7, 4, 2, 1) if depth % (256 * c) == 0 or c == 1)
     sub, deep = tok // halves, depth // chunks
     hbm = pl.BlockSpec(memory_space=pltpu.HBM)
     vmem = pl.BlockSpec(memory_space=pltpu.VMEM)
@@ -234,7 +233,7 @@
             pltpu.VMEM((chunks, deep, width_out), BF16),
             pltpu.VMEM(prior_cov.shape, F32),
             pltpu.VMEM((seqs * width_out, tiles * rows), BF16),
-            pltpu.VMEM((seqs * sub, width_out), F32),
+            pltpu.VMEM((seqs * tok, width_out), F32),
             pltpu.VMEM((halves, sub, tiles * rows), F32),
             pltpu.VMEM((others, halves, sub, tiles * rows), F32),
             pltpu.VMEM((halves, sub, 2 * seqs * width_in), BF16),
@@ -242,7 +241,7 @@
             pltpu.VMEM((group - 1, here, rows, width_in), F32),
             pltpu.VMEM((2, 3 * seqs, block_size), F32),
             pltpu.SemaphoreType.DMA((chunks,)),
-            pltpu.SemaphoreType.DMA((halves, chunks)),
+            pltpu.SemaphoreType.DMA((chunks,)),
             pltpu.SemaphoreType.DMA((halves,)),
             pltpu.SemaphoreType.DMA((4,)),
             pltpu.SemaphoreType.DMA((others, halves)),

time: 17 us -> 17.2 us (1.012)
  Pallas kernels: 16.1 us -> 16.3 us
    pallas_call x1, Pallas kernels: 16.1 us -> 16.3 us  [body(): pl.pallas_call(functools.partial(kernel, seq_axis, tile_axis), out_shape=...]
where the time goes in v5:
time: 17.2 us; the launch traced here: 17.1 us
  Pallas kernels  16.3 us (95%)
  local copies, waits for them, and re-layouts  0.71 us (4%)
    pallas_call x1, Pallas kernels, body(): pl.pallas_call(functools.partial(kernel, seq_axis, tile_axis), out_shape=...  16.3 us
    unnamed x1, local copies, waits for them, and re-layouts  0.71 us

profile of v5, /device:TPU:0, one launch (start us, length us, event | category | flops | bytes accessed | tf_op | source)
XLA Modules:
  0.0 17.1 jit_solution(395128731237791086)
XLA Ops:
  0.0 16.3 %grad_tiles.1 = f32[1,256,256]{2,1,0:T(8,128)S(1)} custom-call(s32[4]{0:T(128)} %lengths_hbm.1, s32[2,8]{1,0:T(2,128)} %bitcast.1, bf16[4,192,2048]{2,1,0:T(8,128)(2,1)} %act_hbm.1, bf16[4,192,7168]{2,1,0:T(8,128)(2,1)} %grad_hbm.1, bf16[2048,128]{1,0:T(8,128)(2,1)} %pin_hbm.1, bf16[7168,256]{1,0:T(8,128)(2,1)} %pout_hbm.1, f32[1,256,256]{2,1,0:T(8,128)} %prior_hbm.1), custom_call_target="tpu_custom_call" | custom-call | tf_op jit(solution)/shard_map/grad_tiles/pallas_call | solution.py:222
  16.4 0.7 %copy.9 = f32[1,256,256]{2,1,0:T(8,128)} copy(f32[1,256,256]{2,1,0:T(8,128)S(1)} %grad_tiles.1) | data formatting | bytes 524288

commit v6 on v4

--- a/solution.py
+++ b/solution.py
@@ -26,7 +26,7 @@
     lengths_hbm, map_hbm, act_hbm, grad_hbm, pin_hbm, pout_hbm, prior_hbm,
     out_ref,
     lengths, tile_map, act_v, grad_v, pin_v, pout_v, prior_v,
-    select_v, total_v, picked, picked_in, acts, parts, parts_in, stacked,
+    select_v, chosen_v, total_v, spread, picked, picked_in, acts, parts, parts_in, stacked,
     pout_sem, grad_sem, act_sem, rest_sem, pick_send, pick_recv, part_send, part_recv,
 ):
     seqs, tok, width = act_v.shape
@@ -100,9 +100,7 @@
         length = jnp.where(lane % seqs == s, lengths[s], length)
     scale = lax.rsqrt(length.astype(F32))
     column = lax.broadcasted_iota(jnp.int32, (width_out, lanes), 0)
-    for s in range(seqs):
-        match = jnp.where(column == wanted, 1.0, 0.0) * jnp.where(lane % seqs == s, 1.0, 0.0)
-        select_v[s * width_out : (s + 1) * width_out, :] = match.astype(BF16)
+    select_v[...] = jnp.where(column == wanted, 1.0, 0.0).astype(BF16)
 
     picks = []
     for h in range(halves):
@@ -112,20 +110,15 @@
         def _(k):
             if h == 0:
                 load_pout(k).wait()
+                chosen_v[k] = dot(pout_v[k], select_v[...]).astype(BF16)
             load_grad(h, k).wait()
             block = grad_v[k, :, pl.ds(h * sub, sub)].reshape(seqs * sub, deep)
-            total_v[...] += dot(block, pout_v[k])
-
-        high, low = split_two(total_v[...])
-        stack = jnp.concatenate(
-            [
-                jnp.concatenate([x[s * sub : (s + 1) * sub] for s in range(seqs)], axis=1)
-                for x in (high, low)
-            ],
-            axis=0,
-        )
-        both = dot(stack, select_v[...])
-        picked[h] = both[:sub] + both[sub:]
+            total_v[...] += dot(block, chosen_v[k])
+
+        mine = jnp.zeros((sub, lanes), F32)
+        for s in range(seqs):
+            mine = jnp.where(lane % seqs == s, total_v[s * sub : (s + 1) * sub, :], mine)
+        picked[h] = mine
         if h == 0:
             pl.semaphore_wait(barrier, group - 1)
         for d in range(1, tile_axis):
@@ -144,13 +137,10 @@
     for h in range(halves):
         load_act(h).wait()
         block = act_v[:, pl.ds(h * sub, sub)].reshape(seqs * sub, width)
-        split = split_two(dot(block, pin_v[...]))
-        for j in range(2):
-            for s in range(seqs):
-                at = (j * seqs + s) * width_in
-                acts[h, :, at : at + width_in] = split[j][s * sub : (s + 1) * sub]
-
-    partial = jnp.zeros((lanes, seqs * width_in), F32)
+        acts[h] = jnp.concatenate(split_two(dot(block, pin_v[...])), axis=1)
+
+    own = jnp.zeros((lanes, width_in), F32)
+    row = lax.broadcasted_iota(jnp.int32, (lanes, sub), 0)
     for h in range(halves):
         total = picked[h]
         for d in range(1, tile_axis):
@@ -158,14 +148,14 @@
             total = total + picked_in[d - 1, h]
         position = seq_me * tok + h * sub + lax.broadcasted_iota(jnp.int32, (sub, lanes), 0)
         total = jnp.where(position < length, total * scale, 0.0)
-        high, low = split_two(total.T)
-        both = dot(high, acts[h])
-        partial = partial + both[:, : seqs * width_in] + both[:, seqs * width_in :]
-        partial = partial + dot(low, acts[h, :, : seqs * width_in])
-    row = lax.broadcasted_iota(jnp.int32, (lanes, width_in), 0)
-    own = jnp.zeros((lanes, width_in), F32)
-    for s in range(seqs):
-        own = jnp.where(row % seqs == s, partial[:, s * width_in : (s + 1) * width_in], own)
+        turned = total.T
+        split = [split_two(jnp.where(row % seqs == s, turned, 0.0)) for s in range(seqs)]
+        for j in range(2):
+            for s in range(seqs):
+                spread[j * lanes : (j + 1) * lanes, s * sub : (s + 1) * sub] = split[s][j]
+        both = dot(spread[...], acts[h])
+        own = own + both[:lanes, :width_in]
+        own = own + both[:lanes, width_in:] + both[lanes:, :width_in]
     parts[...] = own.reshape(tiles, rows, width_in)
 
     moves = []
@@ -233,11 +223,13 @@
             pltpu.VMEM(proj_in.shape, BF16),
             pltpu.VMEM((chunks, deep, width_out), BF16),
             pltpu.VMEM(prior_cov.shape, F32),
-            pltpu.VMEM((seqs * width_out, tiles * rows), BF16),
-            pltpu.VMEM((seqs * sub, width_out), F32),
+            pltpu.VMEM((width_out, tiles * rows), BF16),
+            pltpu.VMEM((chunks, deep, tiles * rows), BF16),
+            pltpu.VMEM((seqs * sub, tiles * rows), F32),
+            pltpu.VMEM((2 * tiles * rows, seqs * sub), BF16),
             pltpu.VMEM((halves, sub, tiles * rows), F32),
             pltpu.VMEM((others, halves, sub, tiles * rows), F32),
-            pltpu.VMEM((halves, sub, 2 * seqs * width_in), BF16),
+            pltpu.VMEM((halves, seqs * sub, 2 * width_in), BF16),
             pltpu.VMEM((tiles, rows, width_in), F32),
             pltpu.VMEM((group - 1, here, rows, width_in), F32),
             pltpu.VMEM((2, 3 * seqs, block_size), F32),

time: 17 us -> 19.1 us (1.12)
  Pallas kernels: 16.1 us -> 18.2 us
    pallas_call x1, Pallas kernels: 16.1 us -> 18.2 us  [body(): pl.pallas_call(functools.partial(kernel, seq_axis, tile_axis), out_shape=...]
where the time goes in v6:
time: 19.1 us; the launch traced here: 19 us
  Pallas kernels  18.2 us (95%)
  local copies, waits for them, and re-layouts  0.71 us (4%)
    pallas_call x1, Pallas kernels, body(): pl.pallas_call(functools.partial(kernel, seq_axis, tile_axis), out_shape=...  18.2 us
    unnamed x1, local copies, waits for them, and re-layouts  0.71 us

profile of v6, /device:TPU:0, one launch (start us, length us, event | category | flops | bytes accessed | tf_op | source)
XLA Modules:
  0.0 19.0 jit_solution(12810822016471868691)
XLA Ops:
  0.0 18.2 %grad_tiles.1 = f32[1,256,256]{2,1,0:T(8,128)S(1)} custom-call(s32[4]{0:T(128)} %lengths_hbm.1, s32[2,8]{1,0:T(2,128)} %bitcast.1, bf16[4,192,2048]{2,1,0:T(8,128)(2,1)} %act_hbm.1, bf16[4,192,7168]{2,1,0:T(8,128)(2,1)} %grad_hbm.1, bf16[2048,128]{1,0:T(8,128)(2,1)} %pin_hbm.1, bf16[7168,256]{1,0:T(8,128)(2,1)} %pout_hbm.1, f32[1,256,256]{2,1,0:T(8,128)} %prior_hbm.1), custom_call_target="tpu_custom_call" | custom-call | tf_op jit(solution)/shard_map/grad_tiles/pallas_call | solution.py:213
  18.3 0.7 %copy.9 = f32[1,256,256]{2,1,0:T(8,128)} copy(f32[1,256,256]{2,1,0:T(8,128)S(1)} %grad_tiles.1) | data formatting | bytes 524288

commit v7 on v4

--- a/solution.py
+++ b/solution.py
@@ -30,7 +30,9 @@
     pout_sem, grad_sem, act_sem, rest_sem, pick_send, pick_recv, part_send, part_recv,
 ):
     seqs, tok, width = act_v.shape
-    chunks, deep, width_out = pout_v.shape
+    depth, width_out = pout_v.shape
+    chunks = pout_sem.shape[0]
+    deep = depth // chunks
     halves = act_sem.shape[0]
     sub = tok // halves
     tiles = tile_map.shape[1]
@@ -45,17 +47,15 @@
     tile_me = lax.axis_index("tile")
     me = seq_me * tile_axis + tile_me
 
+    def chunk(k):
+        return pl.ds(pl.multiple_of(k * deep, 128), deep)
+
     def load_pout(k):
-        return pltpu.make_async_copy(
-            pout_hbm.at[pl.ds(pl.multiple_of(k * deep, 128), deep)], pout_v.at[k], pout_sem.at[k]
-        )
+        return pltpu.make_async_copy(pout_hbm.at[chunk(k)], pout_v.at[chunk(k)], pout_sem.at[k])
 
     def load_grad(h, k):
-        return pltpu.make_async_copy(
-            grad_hbm.at[:, pl.ds(h * sub, sub), pl.ds(pl.multiple_of(k * deep, 128), deep)],
-            grad_v.at[k, :, pl.ds(h * sub, sub)],
-            grad_sem.at[h, k],
-        )
+        at = (slice(None), pl.ds(h * sub, sub), chunk(k))
+        return pltpu.make_async_copy(grad_hbm.at[at], grad_v.at[at], grad_sem.at[h, k])
 
     def load_act(h):
         return pltpu.make_async_copy(
@@ -106,15 +106,20 @@
 
     picks = []
     for h in range(halves):
-        total_v[...] = jnp.zeros_like(total_v)
-
-        @pl.loop(0, chunks)
-        def _(k):
-            if h == 0:
+        if h == 0:
+            total_v[...] = jnp.zeros_like(total_v)
+
+            @pl.loop(0, chunks)
+            def _(k):
                 load_pout(k).wait()
-            load_grad(h, k).wait()
-            block = grad_v[k, :, pl.ds(h * sub, sub)].reshape(seqs * sub, deep)
-            total_v[...] += dot(block, pout_v[k])
+                load_grad(0, k).wait()
+                block = grad_v[:, pl.ds(0, sub), chunk(k)].reshape(seqs * sub, deep)
+                total_v[...] += dot(block, pout_v[chunk(k), :])
+        else:
+            for k in range(chunks):
+                load_grad(h, k).wait()
+            block = grad_v[:, pl.ds(h * sub, sub), :].reshape(seqs * sub, depth)
+            total_v[...] = dot(block, pout_v[...])
 
         high, low = split_two(total_v[...])
         stack = jnp.concatenate(
@@ -217,7 +222,7 @@
     others = max(tile_axis - 1, 1)
     halves = 2 if tok % 32 == 0 else 1
     chunks = next(c for c in (4, 2, 1) if depth % (256 * c) == 0 or c == 1)
-    sub, deep = tok // halves, depth // chunks
+    sub = tok // halves
     hbm = pl.BlockSpec(memory_space=pltpu.HBM)
     vmem = pl.BlockSpec(memory_space=pltpu.VMEM)
     return pl.pallas_call(
@@ -229,9 +234,9 @@
             pltpu.SMEM(seq_lengths.shape, jnp.int32),
             pltpu.SMEM(tile_map.shape[::-1], jnp.int32),
             pltpu.VMEM(activations.shape, BF16),
-            pltpu.VMEM((chunks, seqs, tok, deep), BF16),
+            pltpu.VMEM(out_grads.shape, BF16),
             pltpu.VMEM(proj_in.shape, BF16),
-            pltpu.VMEM((chunks, deep, width_out), BF16),
+            pltpu.VMEM(proj_out.shape, BF16),
             pltpu.VMEM(prior_cov.shape, F32),
             pltpu.VMEM((seqs * width_out, tiles * rows), BF16),
             pltpu.VMEM((seqs * sub, width_out), F32),

time: 17 us -> 18.4 us (1.082)
  Pallas kernels: 16.1 us -> 17.5 us
    pallas_call x1, Pallas kernels: 16.1 us -> 17.5 us  [body(): pl.pallas_call(functools.partial(kernel, seq_axis, tile_axis), out_shape=...]
where the time goes in v7:
time: 18.4 us; the launch traced here: 18.2 us
  Pallas kernels  17.5 us (95%)
  local copies, waits for them, and re-layouts  0.71 us (4%)
    pallas_call x1, Pallas kernels, body(): pl.pallas_call(functools.partial(kernel, seq_axis, tile_axis), out_shape=...  17.5 us
    unnamed x1, local copies, waits for them, and re-layouts  0.71 us

profile of v7, /device:TPU:0, one launch (start us, length us, event | category | flops | bytes accessed | tf_op | source)
XLA Modules:
  0.0 18.2 jit_solution(9324311993611970714)
XLA Ops:
  0.0 17.5 %grad_tiles.1 = f32[1,256,256]{2,1,0:T(8,128)S(1)} custom-call(s32[4]{0:T(128)} %lengths_hbm.1, s32[2,8]{1,0:T(2,128)} %bitcast.1, bf16[4,192,2048]{2,1,0:T(8,128)(2,1)} %act_hbm.1, bf16[4,192,7168]{2,1,0:T(8,128)(2,1)} %grad_hbm.1, bf16[2048,128]{1,0:T(8,128)(2,1)} %pin_hbm.1, bf16[7168,256]{1,0:T(8,128)(2,1)} %pout_hbm.1, f32[1,256,256]{2,1,0:T(8,128)} %prior_hbm.1), custom_call_target="tpu_custom_call" | custom-call | tf_op jit(solution)/shard_map/grad_tiles/pallas_call | solution.py:228
  17.5 0.7 %copy.9 = f32[1,256,256]{2,1,0:T(8,128)} copy(f32[1,256,256]{2,1,0:T(8,128)S(1)} %grad_tiles.1) | data formatting | bytes 524288

commit v8 on v4

--- a/solution.py
+++ b/solution.py
@@ -141,7 +141,8 @@
             picks.append(copy)
 
     load_pin.wait()
-    for h in range(halves):
+    @pl.loop(0, halves)
+    def _(h):
         load_act(h).wait()
         block = act_v[:, pl.ds(h * sub, sub)].reshape(seqs * sub, width)
         split = split_two(dot(block, pin_v[...]))

time: 17 us -> 16.9 us (level)
  no operation moved by 1% of the time
where the time goes in v8:
time: 16.9 us; the launch traced here: 16.8 us
  Pallas kernels  16.1 us (95%)
  local copies, waits for them, and re-layouts  0.71 us (4%)
    pallas_call x1, Pallas kernels, body(): pl.pallas_call(functools.partial(kernel, seq_axis, tile_axis), out_shape=...  16.1 us
    unnamed x1, local copies, waits for them, and re-layouts  0.71 us

profile of v8, /device:TPU:0, one launch (start us, length us, event | category | flops | bytes accessed | tf_op | source)
XLA Modules:
  0.0 16.8 jit_solution(10824942242666077920)
XLA Ops:
  0.0 16.1 %grad_tiles.1 = f32[1,256,256]{2,1,0:T(8,128)S(1)} custom-call(s32[4]{0:T(128)} %lengths_hbm.1, s32[2,8]{1,0:T(2,128)} %bitcast.1, bf16[4,192,2048]{2,1,0:T(8,128)(2,1)} %act_hbm.1, bf16[4,192,7168]{2,1,0:T(8,128)(2,1)} %grad_hbm.1, bf16[2048,128]{1,0:T(8,128)(2,1)} %pin_hbm.1, bf16[7168,256]{1,0:T(8,128)(2,1)} %pout_hbm.1, f32[1,256,256]{2,1,0:T(8,128)} %prior_hbm.1), custom_call_target="tpu_custom_call" | custom-call | tf_op jit(solution)/shard_map/grad_tiles/pallas_call | solution.py:224
  16.1 0.7 %copy.9 = f32[1,256,256]{2,1,0:T(8,128)} copy(f32[1,256,256]{2,1,0:T(8,128)S(1)} %grad_tiles.1) | data formatting | bytes 524288
